TPU v7x, 256 devices: a whole 4x4x8 slice. The times are simulated.
256 devices in a mesh: row: 16 (over z, core), col: 16 (over y, x).
Axes of the slice: x: 4, y: 4, z: 8, core: 2. Of those that a mesh axis runs over, the one named last changes fastest.
Arguments:
- tokens: bfloat16 [1024, 12288], P('col', 'row'), may hold values from -6 to 6
- w_in: bfloat16 [12288, 24576], P('row', 'col'), may hold values from -0.0546875 to 0.0546875
- w_out: bfloat16 [24576, 12288], P('col', 'row'), may hold values from -0.0390625 to 0.0390625
- grad_out: bfloat16 [1024, 12288], P('col', 'row'), may hold values from -6 to 6
Outputs:
- layer_out: bfloat16 [1024, 12288], P('col', 'row')
- grad_tokens: bfloat16 [1024, 12288], P('col', 'row')
- grad_w_in: bfloat16 [12288, 24576], P('row', 'col')
- grad_w_out: bfloat16 [24576, 12288], P('col', 'row')
All inputs are finite; a program needn't handle non-finite values.
Results may differ from a plain program's by a relative error of at most 0.0049.
Values may be sent and summed in bfloat16 or wider, within the bound.
A program may use at most 128 MiB of HBM per device.

v0:
```python
import jax
import jax.numpy as jnp
from jax import lax
from jax.sharding import PartitionSpec as P

gelu_coef = 0.7978845608


def gelu_tanh(values):
    tanh_arg = gelu_coef * (values + 0.044715 * values * values * values)
    return 0.5 * values * (1.0 + jnp.tanh(tanh_arg))


def gelu_slope(values):
    tanh_val = jnp.tanh(gelu_coef * (values + 0.044715 * values * values * values))
    return 0.5 * (1.0 + tanh_val) + 0.5 * values * (1.0 - tanh_val * tanh_val) * gelu_coef * (
        1.0 + 3.0 * 0.044715 * values * values
    )


def times_plain(left, right):
    return jnp.dot(left, right, preferred_element_type=jnp.float32)


def times_transposed(left, right):
    return lax.dot_general(
        left, right, (((1,), (1,)), ((), ())), preferred_element_type=jnp.float32
    )


def over_tokens(left, right):
    return lax.dot_general(
        left, right, (((0,), (0,)), ((), ())), preferred_element_type=jnp.float32
    )


def body(tokens, w_in, w_out, grad_out):
    all_tokens = lax.all_gather(tokens, "col", axis=0, tiled=True)
    all_grads = lax.all_gather(grad_out, "col", axis=0, tiled=True)
    hidden = lax.psum_scatter(times_plain(all_tokens, w_in), "row", scatter_dimension=0, tiled=True)
    activation = gelu_tanh(hidden).astype(jnp.bfloat16)
    all_act = lax.all_gather(activation, "row", axis=0, tiled=True)
    layer_out = lax.psum_scatter(
        times_plain(all_act, w_out), "col", scatter_dimension=0, tiled=True
    ).astype(jnp.bfloat16)
    grad_w_out = over_tokens(all_act, all_grads).astype(jnp.bfloat16)
    grad_act = lax.psum_scatter(
        times_transposed(all_grads, w_out), "row", scatter_dimension=0, tiled=True
    )
    grad_hidden = (grad_act * gelu_slope(hidden)).astype(jnp.bfloat16)
    all_grad_hidden = lax.all_gather(grad_hidden, "row", axis=0, tiled=True)
    grad_w_in = over_tokens(all_tokens, all_grad_hidden).astype(jnp.bfloat16)
    grad_tokens = lax.psum_scatter(
        times_transposed(all_grad_hidden, w_in), "col", scatter_dimension=0, tiled=True
    ).astype(jnp.bfloat16)
    return (layer_out, grad_tokens, grad_w_in, grad_w_out)


def solution(mesh):
    placed = (P("col", "row"), P("row", "col"), P("col", "row"), P("col", "row"))
    return jax.shard_map(
        body,
        mesh=mesh,
        in_specs=placed,
        out_specs=(P("col", "row"), P("col", "row"), P("row", "col"), P("col", "row")),
        check_vma=False,
    )
```

profile of v0, /device:TPU:32, one launch (start us, length us, event | category | flops | bytes accessed | tf_op | source)
XLA Modules:
  0.0 508.3 jit_solution(6853283657797447159)
XLA Ops:
  7.2 0.0 copy-start
  7.2 0.0 all-gather.9.cloned.1.call-start
  7.2 0.7 all-gather.9.cloned.1.call-update
  7.9 0.0 all-gather.5.cloned.1.call-start
  8.0 0.7 all-gather.5.cloned.1.call-update
  8.7 0.0 reduce-scatter.9.cloned.1.call-start
  8.7 53.3 %all-gather.9.cloned.1.call-done = bf16[1024,768]{1,0:T(8,128)(2,1)} async-done(((bf16[64,768]{1,0:T(8,128)(2,1)}), bf16[1024,768]{1,0:T(8,128)(2,1)}) %all-gather.9.cloned.1.call-update) | async-done | bytes 1572880 | tf_op jit(solution)/shard_map/all_gather | solution.py:39
  62.0 0.0 copy-done
  62.0 6.0 %fusion.10 = f32[1024,1536]{1,0:T(8,128)} fusion(bf16[1024,768]{1,0:T(8,128)(2,1)} %all-gather.9.cloned.1.call-done, bf16[1536,768]{1,0:T(8,128)(2,1)S(1)} %copy-done), kind=kOutput, calls=%fused_computation.15 | convolution fusion | flops 2415919104 | bytes 10223616 | tf_op jit(solution)/shard_map/dot_general | solution.py:26
  68.0 0.0 reduce-scatter.9.cloned.1.call-update
  68.0 0.0 reduce-scatter.5.cloned.1.call-start
  68.1 44.8 %all-gather.5.cloned.1.call-done = bf16[1024,768]{1,0:T(8,128)(2,1)} async-done(((bf16[64,768]{1,0:T(8,128)(2,1)}), bf16[1024,768]{1,0:T(8,128)(2,1)}) %all-gather.5.cloned.1.call-update) | async-done | bytes 1572880 | tf_op jit(solution)/shard_map/all_gather | solution.py:38
  112.9 7.4 %fusion.8 = f32[1024,1536]{1,0:T(8,128)} fusion(bf16[1024,768]{1,0:T(8,128)(2,1)} %all-gather.5.cloned.1.call-done, bf16[768,1536]{1,0:T(8,128)(2,1)} %param.5), kind=kOutput, calls=%fused_computation.13 | convolution fusion | flops 2415919104 | bytes 10223616 | tf_op jit(solution)/shard_map/dot_general | solution.py:22
  120.3 0.0 reduce-scatter.5.cloned.1.call-update
  120.3 0.0 all-gather.7.cloned.1.call-start
  120.3 57.8 %reduce-scatter.9.cloned.1.call-done = f32[64,1536]{1,0:T(8,128)} async-done(((f32[1024,1536]{1,0:T(8,128)}), f32[64,1536]{1,0:T(8,128)}) %reduce-scatter.9.cloned.1.call-update) | async-done | bytes 393232 | tf_op jit(solution)/shard_map/reduce_scatter | solution.py:47
  178.1 67.7 %reduce-scatter.5.cloned.1.call-done = f32[64,1536]{1,0:T(8,128)} async-done(((f32[1024,1536]{1,0:T(8,128)}), f32[64,1536]{1,0:T(8,128)}) %reduce-scatter.5.cloned.1.call-update) | async-done | bytes 393232 | tf_op jit(solution)/shard_map/reduce_scatter | solution.py:40
  245.7 2.1 fusion.7
  247.9 0.0 all-gather.7.cloned.1.call-update
  247.9 0.0 all-gather.11.cloned.1.call-start
  247.9 0.5 all-gather.11.cloned.1.call-update
  248.5 0.0 reduce-scatter.7.cloned.1.call-start
  248.5 42.2 %all-gather.7.cloned.1.call-done = bf16[1024,1536]{1,0:T(8,128)(2,1)} async-done(((bf16[64,1536]{1,0:T(8,128)(2,1)}), bf16[1024,1536]{1,0:T(8,128)(2,1)}) %all-gather.7.cloned.1.call-update) | async-done | bytes 3145744 | tf_op jit(solution)/shard_map/all_gather | solution.py:42
  290.8 6.2 %fusion.9 = f32[1024,768]{1,0:T(8,128)} fusion(bf16[1024,1536]{1,0:T(8,128)(2,1)} %all-gather.7.cloned.1.call-done, bf16[1536,768]{1,0:T(8,128)(2,1)S(1)} %copy-done), kind=kOutput, calls=%fused_computation.14 | convolution fusion | flops 2415919104 | bytes 8650752 | tf_op jit(solution)/shard_map/dot_general | solution.py:22
  296.9 0.0 reduce-scatter.7.cloned.1.call-update
  296.9 0.2 reduce-scatter.11.cloned.1.call-start
  297.2 35.5 %all-gather.11.cloned.1.call-done = bf16[1024,1536]{1,0:T(8,128)(2,1)} async-done(((bf16[64,1536]{1,0:T(8,128)(2,1)}), bf16[1024,1536]{1,0:T(8,128)(2,1)}) %all-gather.11.cloned.1.call-update) | async-done | bytes 3145744 | tf_op jit(solution)/shard_map/all_gather | solution.py:51
  332.7 7.0 %fusion.11 = f32[1024,768]{1,0:T(8,128)} fusion(bf16[1024,1536]{1,0:T(8,128)(2,1)} %all-gather.11.cloned.1.call-done, bf16[768,1536]{1,0:T(8,128)(2,1)} %param.5), kind=kOutput, calls=%fused_computation.16 | convolution fusion | flops 2415919104 | bytes 8650752 | tf_op jit(solution)/shard_map/dot_general | solution.py:26
  339.6 0.0 reduce-scatter.11.cloned.1.call-update
  339.7 6.4 %fusion = bf16[768,1536]{0,1:T(8,128)(2,1)} fusion(bf16[1024,1536]{1,0:T(8,128)(2,1)} %all-gather.11.cloned.1.call-done, bf16[1024,768]{1,0:T(8,128)(2,1)} %all-gather.5.cloned.1.call-done), kind=kOutput, calls=%fused_computation.2 | convolution fusion | flops 2417098752 | bytes 7077888 | tf_op jit(solution)/shard_map/dot_general | solution.py:32
  346.1 4.3 copy.8
  350.4 6.5 %convolution_convert_fusion = bf16[1536,768]{1,0:T(8,128)(2,1)} fusion(bf16[1024,1536]{1,0:T(8,128)(2,1)} %all-gather.7.cloned.1.call-done, bf16[1024,768]{1,0:T(8,128)(2,1)} %all-gather.9.cloned.1.call-done), kind=kOutput, calls=%fused_computation | convolution fusion | flops 2417098752 | bytes 7077888 | tf_op jit(solution)/shard_map/dot_general | solution.py:32
  356.9 59.2 %reduce-scatter.7.cloned.1.call-done = f32[64,768]{1,0:T(8,128)} async-done(((f32[1024,768]{1,0:T(8,128)}), f32[64,768]{1,0:T(8,128)}) %reduce-scatter.7.cloned.1.call-update) | async-done | bytes 196624 | tf_op jit(solution)/shard_map/reduce_scatter | solution.py:43
  416.1 1.6 convert_element_type.22
  417.6 82.2 %reduce-scatter.11.cloned.1.call-done = f32[64,768]{1,0:T(8,128)} async-done(((f32[1024,768]{1,0:T(8,128)}), f32[64,768]{1,0:T(8,128)}) %reduce-scatter.11.cloned.1.call-update) | async-done | bytes 196624 | tf_op jit(solution)/shard_map/reduce_scatter | solution.py:53
  499.9 1.6 convert_element_type.24
Async XLA Ops:
  7.2 54.9 %copy-start = (bf16[1536,768]{1,0:T(8,128)(2,1)S(1)}, bf16[1536,768]{1,0:T(8,128)(2,1)}, u32[]{:S(2)}) copy-start(bf16[1536,768]{1,0:T(8,128)(2,1)} %param.6) | copy-start | bytes 7077892
  7.2 54.9 %all-gather.9.cloned.1.call-start = ((), (), s32[]{:S(2)}) async-start(), calls=%async_computation.8 | async-start | bytes 1671168 | tf_op jit(solution)/shard_map/all_gather | solution.py:39
  7.9 105.0 %all-gather.5.cloned.1.call-start = ((), (), s32[]{:S(2)}) async-start(), calls=%async_computation.4 | async-start | bytes 1671168 | tf_op jit(solution)/shard_map/all_gather | solution.py:38
  8.7 169.4 %reduce-scatter.9.cloned.1.call-start = ((), (), s32[]{:S(2)}) async-start(), calls=%async_computation.9 | async-start | bytes 6684672 | tf_op jit(solution)/shard_map/reduce_scatter | solution.py:47
  68.0 177.7 %reduce-scatter.5.cloned.1.call-start = ((), (), s32[]{:S(2)}) async-start(), calls=%async_computation.5 | async-start | bytes 6684672 | tf_op jit(solution)/shard_map/reduce_scatter | solution.py:40
  120.3 170.5 %all-gather.7.cloned.1.call-start = ((), (), s32[]{:S(2)}) async-start(), calls=%async_computation.6 | async-start | bytes 3342336 | tf_op jit(solution)/shard_map/all_gather | solution.py:42
  247.9 84.8 %all-gather.11.cloned.1.call-start = ((), (), s32[]{:S(2)}) async-start(), calls=%async_computation.10 | async-start | bytes 3342336 | tf_op jit(solution)/shard_map/all_gather | solution.py:51
  248.5 167.6 %reduce-scatter.7.cloned.1.call-start = ((), (), s32[]{:S(2)}) async-start(), calls=%async_computation.7 | async-start | bytes 3342336 | tf_op jit(solution)/shard_map/reduce_scatter | solution.py:43
  296.9 203.0 %reduce-scatter.11.cloned.1.call-start = ((), (), s32[]{:S(2)}) async-start(), calls=%async_computation.11 | async-start | bytes 3342336 | tf_op jit(solution)/shard_map/reduce_scatter | solution.py:53
Sparse Core Ops, SparseCore 0:
  10.4 51.5 all-gather.8
  64.5 48.3 all-gather.4
  115.4 62.6 reduce-scatter.8
  180.5 65.2 reduce-scatter.4
  248.0 42.6 all-gather.6
  293.0 39.5 all-gather.10
  336.3 79.7 reduce-scatter.6
  419.7 80.1 reduce-scatter.10
where the time goes:
time: 509 us; the launch traced here: 508 us
  waiting for transfers between devices  445 us (87%)
  matrix products  39.4 us (8%)
  between operations  14.2 us (3%)
  other arithmetic  5.28 us (1%)
    reduce_scatter x1, waiting for transfers between devices, body(): lax.psum_scatter(times_transposed(all_grad_hidden, w_in), 'col', scatter_...  82.2 us
    reduce_scatter x1, waiting for transfers between devices, body(): lax.psum_scatter(times_plain(all_tokens, w_in), 'row', scatter_dimension=...  67.7 us
    reduce_scatter x1, waiting for transfers between devices, body(): lax.psum_scatter(times_plain(all_act, w_out), 'col', scatter_dimension=0,...  59.2 us
    reduce_scatter x1, waiting for transfers between devices, body(): lax.psum_scatter(times_transposed(all_grads, w_out), 'row', scatter_dimen...  57.8 us
    all_gather x1, waiting for transfers between devices, body(): all_grads = lax.all_gather(grad_out, 'col', axis=0, tiled=True)  53.3 us
    all_gather x1, waiting for transfers between devices, body(): all_tokens = lax.all_gather(tokens, 'col', axis=0, tiled=True)  44.8 us
    all_gather x1, waiting for transfers between devices, body(): all_act = lax.all_gather(activation, 'row', axis=0, tiled=True)  42.2 us
    all_gather x1, waiting for transfers between devices, body(): all_grad_hidden = lax.all_gather(grad_hidden, 'row', axis=0, tiled=True)  35.5 us
  transfers between devices with their start and end apart: 8, of which 8 were waited for; matrix products, arithmetic and copies ran while one was open for 9% of the time, Pallas kernels for 0%

commit v1 on v0

v1 whole, which is shorter than its diff:
```python
import jax
import jax.numpy as jnp
from jax import lax
from jax.experimental import pallas as pl
from jax.experimental.pallas import tpu as pltpu
from jax.sharding import PartitionSpec as P

MESH = pl.DeviceIdType.MESH
BF = jnp.bfloat16
F32 = jnp.float32
gelu_coef = 0.7978845608

WAVES = 4
WROWS = 256
CH = 32
HALF = 768
TILE = 256


def wave_pieces():
    first = [(0, 0, 0, 64)]
    first += [(0, d, 0, 32) for d in (1, 3, 2)] + [(d, 0, 0, 32) for d in (1, 3, 2)]
    second = [(1, 3, 0, 64), (3, 1, 0, 64), (1, 1, 32, 32), (3, 3, 32, 32), (2, 2, 0, 64)]
    third = [(1, 2, 0, 64), (2, 1, 0, 64), (3, 2, 0, 64), (2, 3, 0, 64)]
    fourth = [(0, d, 32, 32) for d in (1, 3, 2)] + [(d, 0, 32, 32) for d in (1, 3, 2)]
    fourth += [(1, 1, 0, 32), (3, 3, 0, 32)]
    waves = []
    for pieces in (first, second, third, fourth):
        at, wave = 0, []
        for dy, dx, row0, rows in pieces:
            wave.append((dy, dx, row0, rows, at))
            at += rows
        waves.append(wave)
    return waves


PIECES = wave_pieces()
SENT_ROWS = [192, 256, 256, 256]


def gelu_and_slope(h):
    t = jnp.tanh(gelu_coef * (h + 0.044715 * h * h * h))
    act = 0.5 * h * (1.0 + t)
    slope = 0.5 * (1.0 + t) + 0.5 * h * (1.0 - t * t) * gelu_coef * (1.0 + 3.0 * 0.044715 * h * h)
    return act, slope


def dot_nn(a, b):
    return lax.dot_general(a, b, (((1,), (0,)), ((), ())), preferred_element_type=F32)


def dot_nt(a, b):
    return lax.dot_general(a, b, (((1,), (1,)), ((), ())), preferred_element_type=F32)


def dot_tn(a, b):
    return lax.dot_general(a, b, (((0,), (0,)), ((), ())), preferred_element_type=F32)


def kernel(
    tok_hbm, win_hbm, wout_hbm, gout_hbm,
    lo_hbm, gt_hbm, gwi_hbm, gwo_hbm,
    tg, w_in, w_out, pown, px, pr, sb, rb, ag, ob, outr, gwi, gwo, fin,
    loc_sem, a_ss, a_rs, px_ss, px_rs, rs_ss, rs_rs, ag_ss, ag_rs, x_ss, x_rs, o_ss, o_rs, out_sem,
):
    row, col = lax.axis_index("row"), lax.axis_index("col")
    z, c = row // 2, row % 2
    y, x = col // 4, col % 4
    sign = 1 - 2 * c

    def z_chip(d):
        return (z + d + 16) % 8

    fwd = (z_chip(sign) * 2 + c, col)
    back = (z_chip(-sign) * 2 + c, col)
    mate = (z * 2 + 1 - c, col)

    def plane(dy, dx):
        return (row, ((y + dy + 4) % 4) * 4 + (x + dx + 4) % 4)

    loads = [
        pltpu.make_async_copy(tok_hbm, tg.at[0, 0, pl.ds(0, 64)], loc_sem.at[0]),
        pltpu.make_async_copy(gout_hbm, tg.at[1, 0, pl.ds(0, 64)], loc_sem.at[1]),
        pltpu.make_async_copy(win_hbm, w_in, loc_sem.at[2]),
        pltpu.make_async_copy(wout_hbm, w_out, loc_sem.at[3]),
    ]
    for load in loads:
        load.start()

    barrier = pltpu.get_barrier_semaphore()
    greet = [fwd, back, mate] + [plane(d // 4, d % 4) for d in range(1, 16)]
    for dev in greet:
        pl.semaphore_signal(barrier, inc=1, device_id=dev, device_id_type=MESH)
    loads[0].wait()
    loads[1].wait()
    pl.semaphore_wait(barrier, len(greet))

    def remote(src, dst, ss, rs, dev):
        return pltpu.make_async_remote_copy(
            src_ref=src, dst_ref=dst, send_sem=ss, recv_sem=rs, device_id=dev, device_id_type=MESH
        )

    def wait_bytes(ref, sem):
        pltpu.make_async_copy(ref, ref, sem).wait()

    def push_a(w, arr):
        for dy, dx, row0, rows, at in PIECES[w]:
            if dy or dx:
                remote(
                    tg.at[arr, 0, pl.ds(row0, rows)],
                    tg.at[arr, w, pl.ds(at, rows)],
                    a_ss.at[arr, w],
                    a_rs.at[arr, w],
                    plane(-dy, -dx),
                ).start()

    def wait_a(w, arr):
        wait_bytes(tg.at[arr, w, pl.ds(WROWS - SENT_ROWS[w], SENT_ROWS[w])], a_rs.at[arr, w])

    def partial(w, op):
        def tile(start):
            if op == 0:
                return dot_nn(tg[0, w], w_in[:, pl.ds(start, TILE)])
            return dot_nt(tg[1, w], w_out[pl.ds(start, TILE), :])

        def theirs(j, carry):
            at = pl.multiple_of(j * TILE, TILE)
            px[w, op, :, pl.ds(at, TILE)] = tile(pl.multiple_of((1 - c) * HALF + at, TILE))
            return carry

        def mine(j, carry):
            at = pl.multiple_of(j * TILE, TILE)
            pown[w % 2, op, :, pl.ds(at, TILE)] = tile(pl.multiple_of(c * HALF + at, TILE))
            return carry

        lax.fori_loop(0, HALF // TILE, theirs, 0)
        remote(px.at[w, op], pr.at[w, op], px_ss.at[w, op], px_rs.at[w, op], mate).start()
        lax.fori_loop(0, HALF // TILE, mine, 0)

    def wait_px(w, op):
        wait_bytes(pr.at[w, op], px_rs.at[w, op])

    def own_term(w, op, k):
        rows = pl.ds(pl.multiple_of(k * CH, CH), CH)
        return pown[w % 2, op, rows, :] + pr[w, op, rows, :]

    def rs_send(w, op, n):
        k = z_chip(sign * (4 - n)) if n < 4 else z_chip(-sign * (7 - n))
        term = own_term(w, op, k)
        if n not in (0, 4):
            wait_bytes(rb.at[w, op, n - 1], rs_rs.at[w, op, n - 1])
            term = term + rb[w, op, n - 1].astype(F32)
        sb[w, op, n] = term.astype(BF)
        remote(
            sb.at[w, op, n], rb.at[w, op, n], rs_ss.at[w, op], rs_rs.at[w, op, n], fwd if n < 4 else back
        ).start()

    def rs_final(w, op):
        total = own_term(w, op, z)
        for n in (6, 3):
            wait_bytes(rb.at[w, op, n], rs_rs.at[w, op, n])
            total = total + rb[w, op, n].astype(F32)
        return total

    def ag_slot(w, op, k):
        return ag.at[op, w, c, pl.ds(pl.multiple_of(k * CH, CH), CH)]

    def finish_hidden(w):
        hidden = rs_final(w, 0)
        act, slope = gelu_and_slope(hidden)
        rows = pl.ds(pl.multiple_of(z * CH, CH), CH)
        ag[0, w, c, rows, :] = act.astype(BF)
        ag[1, w, c, rows, :] = (rs_final(w, 1) * slope).astype(BF)

    def ag_wait(w, op, n):
        wait_bytes(sb.at[w, op, n], ag_rs.at[w, op, n])

    def ag_send(w, op, n):
        k = z_chip(-sign * n) if n < 4 else z_chip(sign * (n - 4))
        if n not in (0, 4):
            ag_wait(w, op, n - 1)
        slot = ag_slot(w, op, k)
        remote(slot, slot, ag_ss.at[w, op], ag_rs.at[w, op, n], fwd if n < 4 else back).start()

    def x_send(w, op):
        ag_wait(w, op, 6)
        ag_wait(w, op, 3)
        half = ag.at[op, w, c]
        remote(half, half, x_ss.at[w, op], x_rs.at[w, op], mate).start()

    def x_wait(w, op):
        wait_bytes(ag.at[op, w, 1 - c], x_rs.at[w, op])

    def outputs(w, op):
        def tile(j, carry):
            at = pl.ds(pl.multiple_of(j * TILE, TILE), TILE)
            if op == 0:
                total = dot_nn(ag[0, w, 0], w_out[pl.ds(0, HALF), at])
                total += dot_nn(ag[0, w, 1], w_out[pl.ds(HALF, HALF), at])
            else:
                total = dot_nt(ag[1, w, 0], w_in[at, pl.ds(0, HALF)])
                total += dot_nt(ag[1, w, 1], w_in[at, pl.ds(HALF, HALF)])
            ob[w, op, :, at] = total.astype(BF)
            return carry

        lax.fori_loop(0, HALF // TILE, tile, 0)
        for dy, dx, row0, rows, at in PIECES[w]:
            if dy or dx:
                remote(
                    ob.at[w, op, pl.ds(at, rows)],
                    outr.at[op, dy * 4 + dx, pl.ds(row0, rows)],
                    o_ss.at[w, op],
                    o_rs.at[w, op],
                    plane(dy, dx),
                ).start()

    def phase(p):
        rs, gather = p < WAVES, p >= 1
        for s in range(4):
            for op in range(2):
                if rs:
                    if s == 0:
                        wait_px(p, op)
                    rs_send(p, op, s)
                    if s < 3:
                        rs_send(p, op, 4 + s)
            if gather:
                for op in range(2):
                    ag_send(p - 1, op, s)
                    if s < 3:
                        ag_send(p - 1, op, 4 + s)
            if s == 0 and p + 1 < WAVES:
                wait_a(p + 1, 0)
                wait_a(p + 1, 1)
                if p + 2 < WAVES:
                    push_a(p + 2, 0)
                    push_a(p + 2, 1)
                partial(p + 1, 0)
            if s == 1 and p + 1 < WAVES:
                partial(p + 1, 1)
            if s >= 2 and p >= 2:
                x_wait(p - 2, s - 2)
                outputs(p - 2, s - 2)
        if rs:
            finish_hidden(p)
        if gather:
            x_send(p - 1, 0)
            x_send(p - 1, 1)

    push_a(0, 0)
    push_a(0, 1)
    loads[2].wait()
    loads[3].wait()
    wait_a(0, 0)
    push_a(1, 0)
    partial(0, 0)
    wait_a(0, 1)
    push_a(1, 1)
    partial(0, 1)
    for p in range(WAVES + 1):
        phase(p)
    last = WAVES - 1
    for op in range(2):
        x_wait(last, op)
        outputs(last, op)

    def grad_w_out(i, carry):
        hf, j = i // 3, i % 3
        units = pl.ds(pl.multiple_of(j * TILE, TILE), TILE)
        total = dot_tn(ag[0, 0, hf, :, units], tg[1, 0])
        for w in range(1, WAVES):
            total += dot_tn(ag[0, w, hf, :, units], tg[1, w])
        rows = pl.ds(pl.multiple_of(i * TILE, TILE), TILE)
        gwo[rows, :] = total.astype(BF)
        return carry

    def grad_w_in(i, carry):
        hf, j = i // 3, i % 3
        units = pl.ds(pl.multiple_of(j * TILE, TILE), TILE)
        total = dot_tn(tg[0, 0, :, units], ag[1, 0, hf])
        for w in range(1, WAVES):
            total += dot_tn(tg[0, w, :, units], ag[1, w, hf])
        gwi[units, pl.ds(pl.multiple_of(hf * HALF, HALF), HALF)] = total.astype(BF)
        return carry

    lax.fori_loop(0, 6, grad_w_out, 0)
    put_gwo = pltpu.make_async_copy(gwo, gwo_hbm, out_sem.at[0])
    put_gwo.start()
    lax.fori_loop(0, 6, grad_w_in, 0)
    put_gwi = pltpu.make_async_copy(gwi, gwi_hbm, out_sem.at[1])
    put_gwi.start()

    puts = [put_gwo, put_gwi]
    for op, out in ((0, lo_hbm), (1, gt_hbm)):
        for w in range(WAVES):
            wait_bytes(ob.at[w, op, pl.ds(WROWS - SENT_ROWS[w], SENT_ROWS[w])], o_rs.at[w, op])

        def add_up(i, carry, op=op):
            rows = pl.ds(pl.multiple_of(i * 16, 16), 16)
            total = ob[0, op, rows, :].astype(F32)
            for slot in range(1, 16):
                total = total + outr[op, slot, rows, :].astype(F32)
            fin[op, rows, :] = total.astype(BF)
            return carry

        lax.fori_loop(0, 4, add_up, 0)
        put = pltpu.make_async_copy(fin.at[op], out, out_sem.at[2 + op])
        put.start()
        puts.append(put)

    for w in range(WAVES):
        sent = pl.ds(WROWS - SENT_ROWS[w], SENT_ROWS[w])
        for op in range(2):
            wait_bytes(tg.at[op, w, sent], a_ss.at[op, w])
            wait_bytes(px.at[w, op], px_ss.at[w, op])
            wait_bytes(sb.at[w, op], rs_ss.at[w, op])
            wait_bytes(sb.at[w, op], ag_ss.at[w, op])
            wait_bytes(ag.at[op, w, c], x_ss.at[w, op])
            wait_bytes(ob.at[w, op, sent], o_ss.at[w, op])
    for put in puts:
        put.wait()


def body(tokens, w_in, w_out, grad_out):
    dma = pltpu.SemaphoreType.DMA
    any_spec = pl.BlockSpec(memory_space=pl.ANY)
    return pl.pallas_call(
        kernel,
        name="ffn",
        out_shape=(
            jax.ShapeDtypeStruct((64, HALF), BF),
            jax.ShapeDtypeStruct((64, HALF), BF),
            jax.ShapeDtypeStruct((HALF, 2 * HALF), BF),
            jax.ShapeDtypeStruct((2 * HALF, HALF), BF),
        ),
        in_specs=[any_spec] * 4,
        out_specs=[any_spec] * 4,
        scratch_shapes=[
            pltpu.VMEM((2, WAVES, WROWS, HALF), BF),
            pltpu.VMEM((HALF, 2 * HALF), BF),
            pltpu.VMEM((2 * HALF, HALF), BF),
            pltpu.VMEM((2, 2, WROWS, HALF), F32),
            pltpu.VMEM((WAVES, 2, WROWS, HALF), F32),
            pltpu.VMEM((WAVES, 2, WROWS, HALF), F32),
            pltpu.VMEM((WAVES, 2, 7, CH, HALF), BF),
            pltpu.VMEM((WAVES, 2, 7, CH, HALF), BF),
            pltpu.VMEM((2, WAVES, 2, WROWS, HALF), BF),
            pltpu.VMEM((WAVES, 2, WROWS, HALF), BF),
            pltpu.VMEM((2, 16, 64, HALF), BF),
            pltpu.VMEM((HALF, 2 * HALF), BF),
            pltpu.VMEM((2 * HALF, HALF), BF),
            pltpu.VMEM((2, 64, HALF), BF),
            dma((4,)),
            dma((2, WAVES)), dma((2, WAVES)),
            dma((WAVES, 2)), dma((WAVES, 2)),
            dma((WAVES, 2)), dma((WAVES, 2, 7)),
            dma((WAVES, 2)), dma((WAVES, 2, 7)),
            dma((WAVES, 2)), dma((WAVES, 2)),
            dma((WAVES, 2)), dma((WAVES, 2)),
            dma((4,)),
        ],
        compiler_params=pltpu.CompilerParams(
            collective_id=0, has_side_effects=True, vmem_limit_bytes=60 << 20
        ),
        cost_estimate=pl.CostEstimate(flops=14500000000, bytes_accessed=10000000, transcendentals=2000000),
    )(tokens, w_in, w_out, grad_out)


def solution(mesh):
    placed = (P("col", "row"), P("row", "col"), P("col", "row"), P("col", "row"))
    return jax.shard_map(
        body,
        mesh=mesh,
        in_specs=placed,
        out_specs=(P("col", "row"), P("col", "row"), P("row", "col"), P("col", "row")),
        check_vma=False,
    )
```

time: 509 us -> 136 us (0.27)
  waiting for transfers between devices: 445 us -> 0 us
  Pallas kernels: 0 us -> 126 us
  matrix products: 39.4 us -> 0 us
  between operations: 14.2 us -> 0.64 us
  other arithmetic: 5.28 us -> 0 us
    reduce_scatter x4 -> x0, waiting for transfers between devices: 267 us -> none  [the longest x1 82.2 us: body(): lax.psum_scatter(times_transposed(all_grad_hidden, w_in), 'col', scatter_...]
    all_gather x4 -> x0, waiting for transfers between devices: 176 us -> none  [the longest x1 53.3 us: body(): all_grads = lax.all_gather(grad_out, 'col', axis=0, tiled=True)]
    pallas_call x0 -> x1, Pallas kernels: none -> 126 us  [body(): pl.pallas_call(kernel, name='ffn', out_shape=(jax.ShapeDtypeStruct((64, H...]
    dot_general x6 -> x0, matrix products: 39.4 us -> none  [the longest x2 13.5 us: times_plain(): return jnp.dot(left, right, preferred_element_type=jnp.float32)]
    convert_element_type x3 -> x0, other arithmetic: 5.28 us -> none  [the longest x1 2.12 us: body(): grad_hidden = (grad_act * gelu_slope(hidden)).astype(jnp.bfloat16)]
  transfers between devices with their start and end apart: 8 -> 0, of which waited for: 8 -> 0; matrix products, arithmetic and copies ran while one was open for 9% -> 0% of each run, Pallas kernels for 0% -> 0%
where the time goes in v1:
time: 136 us; the launch traced here: 135 us
  Pallas kernels  126 us (93%)
  local copies, waits for them, and re-layouts  7.86 us (6%)
    pallas_call x1, Pallas kernels, body(): pl.pallas_call(kernel, name='ffn', out_shape=(jax.ShapeDtypeStruct((64, H...  126 us
    unnamed x6, local copies, waits for them, and re-layouts  7.86 us

profile of v1, /device:TPU:32, one launch (start us, length us, event | category | flops | bytes accessed | tf_op | source)
XLA Modules:
  0.0 134.6 jit_solution(13769894881801006486)
XLA Ops:
  0.6 126.0 %ffn.1 = (bf16[64,768]{1,0:T(8,128)(2,1)}, bf16[64,768]{1,0:T(8,128)(2,1)}, bf16[768,1536]{1,0:T(8,128)(2,1)}, bf16[1536,768]{1,0:T(8,128)(2,1)}) custom-call(bf16[64,768]{1,0:T(8,128)(2,1)} %tok_hbm.1, bf16[768,1536]{1,0:T(8,128)(2,1)} %win_hbm.1, bf16[1536,768]{1,0:T(8,128)(2,1)} %wout_hbm.1, bf16[64,768]{1,0:T(8,128)(2,1)} %gout_hbm.1), custom_call_target="tpu_custom_call" | custom-call | flops 14499999744 | bytes 10000000 | tf_op jit(solution)/shard_map/ffn/pallas_call | solution.py:327
  126.7 1.5 %copy.12 = bf16[64,768]{1,0:T(8,128)(2,1)} copy(bf16[64,768]{1,0:T(8,128)(2,1)} %get-tuple-element.8) | data formatting | bytes 196608
  128.2 1.5 %copy.13 = bf16[64,768]{1,0:T(8,128)(2,1)} copy(bf16[64,768]{1,0:T(8,128)(2,1)} %get-tuple-element.9) | data formatting | bytes 196608
  129.8 0.0 copy-start
  129.8 3.4 %copy.14 = bf16[768,1536]{1,0:T(8,128)(2,1)} copy(bf16[768,1536]{1,0:T(8,128)(2,1)} %get-tuple-element.10) | data formatting | bytes 4718592
  133.1 0.0 copy-done
  133.1 1.4 %copy.15 = bf16[1536,768]{1,0:T(8,128)(2,1)} copy(bf16[1536,768]{1,0:T(8,128)(2,1)S(1)} %copy-done) | data formatting | bytes 4718592
Async XLA Ops:
  129.8 3.4 %copy-start = (bf16[1536,768]{1,0:T(8,128)(2,1)S(1)}, bf16[1536,768]{1,0:T(8,128)(2,1)}, u32[]{:S(2)}) copy-start(bf16[1536,768]{1,0:T(8,128)(2,1)} %get-tuple-element.11) | copy-start | bytes 7077892

commit v2 on v0

v2 whole, which is shorter than its diff:
```python
import jax
import jax.numpy as jnp
from jax import lax
from jax.experimental import pallas as pl
from jax.experimental.pallas import tpu as pltpu
from jax.sharding import PartitionSpec as P

MESH = pl.DeviceIdType.MESH
BF = jnp.bfloat16
F32 = jnp.float32
gelu_coef = 0.7978845608

WAVES = 4
ROWS = 256
PART = 16
START = [0, 2, 4, 6]
CH = 32
HALF = 768
TILE = 256


def part_of(dy, dx):
    if dy == 0:
        return PART * dx
    if dx == 0:
        return PART * (3 + dy)
    return PART * (7 + 3 * (dy - 1) + dx - 1)


def gelu_and_slope(h):
    t = jnp.tanh(gelu_coef * (h + 0.044715 * h * h * h))
    act = 0.5 * h * (1.0 + t)
    slope = 0.5 * (1.0 + t) + 0.5 * h * (1.0 - t * t) * gelu_coef * (1.0 + 3.0 * 0.044715 * h * h)
    return act, slope


def dot_nn(a, b):
    return lax.dot_general(a, b, (((1,), (0,)), ((), ())), preferred_element_type=F32)


def dot_nt(a, b):
    return lax.dot_general(a, b, (((1,), (1,)), ((), ())), preferred_element_type=F32)


def dot_tn(a, b):
    return lax.dot_general(a, b, (((0,), (0,)), ((), ())), preferred_element_type=F32)


def kernel(
    tok_hbm, win_hbm, wout_hbm, gout_hbm,
    lo, gt, gwi, gwo,
    shard, tg, w_in, w_out, pown, px, pr, sb, rb, ag, ob, outr,
    loc_sem, a_ss, a_rs, r_ss, r_rs, px_ss, px_rs, rs_ss, rs_rs, ag_ss, ag_rs, x_ss, x_rs, o_ss, o_rs,
):
    row, col = lax.axis_index("row"), lax.axis_index("col")
    z, c = row // 2, row % 2
    y, x = col // 4, col % 4
    sign = 1 - 2 * c

    def z_chip(d):
        return (z + d + 16) % 8

    fwd = (z_chip(sign) * 2 + c, col)
    back = (z_chip(-sign) * 2 + c, col)
    mate = (z * 2 + 1 - c, col)

    def plane(dy, dx):
        return (row, ((y + dy + 4) % 4) * 4 + (x + dx + 4) % 4)

    shards = [
        pltpu.make_async_copy(tok_hbm, shard.at[0], loc_sem.at[0]),
        pltpu.make_async_copy(gout_hbm, shard.at[1], loc_sem.at[1]),
    ]
    loads = [
        pltpu.make_async_copy(win_hbm, w_in, loc_sem.at[2]),
        pltpu.make_async_copy(wout_hbm, w_out, loc_sem.at[3]),
    ]
    for load in shards + loads:
        load.start()

    barrier = pltpu.get_barrier_semaphore()
    greet = [fwd, back, mate] + [plane(d // 4, d % 4) for d in range(1, 16)]
    for dev in greet:
        pl.semaphore_signal(barrier, inc=1, device_id=dev, device_id_type=MESH)
    for load in shards:
        load.wait()
    for arr in range(2):
        for w in range(WAVES):
            tg[arr, pl.ds(ROWS * w, PART), :] = shard[arr, pl.ds(PART * w, PART), :]
    pl.semaphore_wait(barrier, len(greet))

    def remote(src, dst, ss, rs, dev):
        return pltpu.make_async_remote_copy(
            src_ref=src, dst_ref=dst, send_sem=ss, recv_sem=rs, device_id=dev, device_id_type=MESH
        )

    def wait_bytes(ref, sem):
        pltpu.make_async_copy(ref, ref, sem).wait()

    def push_cross(w, arr):
        for dy, dx in ((0, 1), (1, 0), (0, 3), (3, 0), (0, 2), (2, 0)):
            remote(
                shard.at[arr, pl.ds(PART * w, PART)],
                tg.at[arr, pl.ds(ROWS * w + part_of(dy, dx), PART)],
                a_ss.at[arr, w],
                a_rs.at[arr, w],
                plane(-dy, -dx),
            ).start()

    def cross_rows(w, arr):
        return tg.at[arr, pl.ds(ROWS * w + PART, 6 * PART)]

    def wait_cross(w, arr):
        wait_bytes(cross_rows(w, arr), a_rs.at[arr, w])

    def push_relay(w, arr):
        def send(src, dst, rows, dev):
            remote(
                tg.at[arr, pl.ds(ROWS * w + src, rows)],
                tg.at[arr, pl.ds(ROWS * w + dst, rows)],
                r_ss.at[arr, w],
                r_rs.at[arr, w],
                dev,
            ).start()

        for d in (1, 3):
            send(part_of(0, 1), part_of(d, 1), 3 * PART, plane(-d, 0))
            send(part_of(2, 0), part_of(2, d), PART, plane(0, -d))
        send(part_of(2, 0), part_of(2, 2), PART, plane(0, -2))

    def relay_rows(w, arr):
        return tg.at[arr, pl.ds(ROWS * w + 7 * PART, 9 * PART)]

    def wait_relay(w, arr):
        wait_bytes(relay_rows(w, arr), r_rs.at[arr, w])

    def forward(w):
        for arr in range(2):
            wait_cross(w, arr)
            push_relay(w, arr)

    def product(w, op, start):
        tokens = tg[op, pl.ds(ROWS * w, ROWS), :]
        if op == 0:
            return dot_nn(tokens, w_in[:, pl.ds(start, TILE)])
        return dot_nt(tokens, w_out[pl.ds(start, TILE), :])

    def px_ref(w, op):
        return px.at[w % 2, op]

    def theirs(w, op):
        if w >= 2:
            wait_bytes(px_ref(w - 2, op), px_ss.at[w - 2, op])

        def tile(j, carry):
            at = pl.multiple_of(j * TILE, TILE)
            px[w % 2, op, :, pl.ds(at, TILE)] = product(
                w, op, pl.multiple_of((1 - c) * HALF + at, TILE)
            )
            return carry

        lax.fori_loop(0, HALF // TILE, tile, 0)
        remote(
            px_ref(w, op), pr.at[op, pl.ds(ROWS * w, ROWS)], px_ss.at[w, op], px_rs.at[w, op], mate
        ).start()

    def mine(w, op):
        def tile(j, carry):
            at = pl.multiple_of(j * TILE, TILE)
            pown[op, pl.ds(ROWS * w, ROWS), pl.ds(at, TILE)] = product(
                w, op, pl.multiple_of(c * HALF + at, TILE)
            )
            return carry

        lax.fori_loop(0, HALF // TILE, tile, 0)

    def wait_px(w, op):
        wait_bytes(pr.at[op, pl.ds(ROWS * w, ROWS)], px_rs.at[w, op])

    def own_term(w, op, k):
        at = pl.multiple_of(k * CH, CH)
        return pown[op, pl.ds(ROWS * w + at, CH), :] + pr[op, pl.ds(ROWS * w + at, CH), :]

    def slot(w, n):
        return pl.ds((7 * w + n) * CH, CH)

    def rs_send(w, op, n):
        k = z_chip(sign * (4 - n)) if n < 4 else z_chip(-sign * (7 - n))
        term = own_term(w, op, k)
        if n not in (0, 4):
            wait_bytes(rb.at[op, slot(w, n - 1)], rs_rs.at[w, op, n - 1])
            term = term + rb[op, slot(w, n - 1), :].astype(F32)
        sb[op, slot(w, n), :] = term.astype(BF)
        remote(
            sb.at[op, slot(w, n)], rb.at[op, slot(w, n)], rs_ss.at[w, op], rs_rs.at[w, op, n],
            fwd if n < 4 else back,
        ).start()

    def rs_final(w, op):
        total = own_term(w, op, z)
        for n in (6, 3):
            wait_bytes(rb.at[op, slot(w, n)], rs_rs.at[w, op, n])
            total = total + rb[op, slot(w, n), :].astype(F32)
        return total

    def chunk(w, k):
        return pl.ds(ROWS * w + pl.multiple_of(k * CH, CH), CH)

    def finish_hidden(w):
        hidden = rs_final(w, 0)
        act, slope = gelu_and_slope(hidden)
        ag[0, c, chunk(w, z), :] = act.astype(BF)
        ag[1, c, chunk(w, z), :] = (rs_final(w, 1) * slope).astype(BF)

    def ag_wait(w, op, n):
        wait_bytes(sb.at[op, slot(w, n)], ag_rs.at[w, op, n])

    def ag_send(w, op, n):
        k = z_chip(-sign * n) if n < 4 else z_chip(sign * (n - 4))
        if n not in (0, 4):
            ag_wait(w, op, n - 1)
        part = ag.at[op, c, chunk(w, k)]
        remote(part, part, ag_ss.at[w, op], ag_rs.at[w, op, n], fwd if n < 4 else back).start()

    def half_ref(w, op, half):
        return ag.at[op, half, pl.ds(ROWS * w, ROWS)]

    def x_send(w, op):
        ag_wait(w, op, 6)
        ag_wait(w, op, 3)
        remote(half_ref(w, op, c), half_ref(w, op, c), x_ss.at[w, op], x_rs.at[w, op], mate).start()

    def x_wait(w, op):
        wait_bytes(half_ref(w, op, 1 - c), x_rs.at[w, op])

    def outputs(w, op):
        tokens = pl.ds(ROWS * w, ROWS)

        def tile(j, carry):
            at = pl.ds(pl.multiple_of(j * TILE, TILE), TILE)
            if op == 0:
                total = dot_nn(ag[0, 0, tokens, :], w_out[pl.ds(0, HALF), at])
                total += dot_nn(ag[0, 1, tokens, :], w_out[pl.ds(HALF, HALF), at])
            else:
                total = dot_nt(ag[1, 0, tokens, :], w_in[at, pl.ds(0, HALF)])
                total += dot_nt(ag[1, 1, tokens, :], w_in[at, pl.ds(HALF, HALF)])
            ob[op, tokens, at] = total.astype(BF)
            return carry

        lax.fori_loop(0, HALF // TILE, tile, 0)
        for n in (4, 1, 12, 3, 8, 2, 5, 15, 7, 13, 6, 9, 14, 11, 10):
            dy, dx = n // 4, n % 4
            remote(
                ob.at[op, pl.ds(ROWS * w + part_of(dy, dx), PART)],
                outr.at[op, n, pl.ds(PART * w, PART)],
                o_ss.at[w, op],
                o_rs.at[w, op],
                plane(dy, dx),
            ).start()

    def o_rows(w, op):
        return ob.at[op, pl.ds(ROWS * w + PART, ROWS - PART)]

    def weight_grad(which, hf):
        def tile(j, carry):
            units = pl.ds(pl.multiple_of(j * TILE, TILE), TILE)
            if which == 0:
                total = dot_tn(ag[0, hf, :, units], tg[1])
                gwo[pl.ds(pl.multiple_of(hf * HALF + j * TILE, TILE), TILE), :] = total.astype(BF)
            else:
                total = dot_tn(tg[0, :, units], ag[1, hf])
                gwi[units, pl.ds(pl.multiple_of(hf * HALF, HALF), HALF)] = total.astype(BF)
            return carry

        lax.fori_loop(0, 3, tile, 0)

    def tick(t):
        ages = [t - START[w] for w in range(WAVES)]
        for w in range(WAVES):
            age = ages[w]
            if 1 <= age <= 3:
                for op in range(2):
                    rs_send(w, op, age)
                    if age < 3:
                        rs_send(w, op, 4 + age)
            if age == 4:
                finish_hidden(w)
            if 4 <= age <= 7:
                for op in range(2):
                    ag_send(w, op, age - 4)
                    if age > 4:
                        ag_send(w, op, age - 1)
            if age == 8:
                x_send(w, 0)
                x_send(w, 1)
        for w in range(WAVES):
            if ages[w] == 0:
                for op in range(2):
                    wait_px(w, op)
                    rs_send(w, op, 0)
                    rs_send(w, op, 4)
        if t in (1, 2):
            forward(t + 1)
        for w in range(1, WAVES):
            if ages[w] == -1:
                for op in range(2):
                    wait_relay(w, op)
                    theirs(w, op)
                mine(w, 0)
                mine(w, 1)
        for w in range(WAVES - 1):
            if ages[w] == 9:
                for op in range(2):
                    x_wait(w, op)
                    outputs(w, op)

    push_cross(0, 0)
    push_cross(0, 1)
    forward(0)
    push_cross(1, 0)
    push_cross(1, 1)
    for load in loads:
        load.wait()
    for op in range(2):
        wait_relay(0, op)
        theirs(0, op)
    forward(1)
    for w in (2, 3):
        push_cross(w, 0)
        push_cross(w, 1)
    mine(0, 0)
    mine(0, 1)
    for t in range(START[-1] + 9):
        tick(t)
    last = WAVES - 1
    weight_grad(0, c)
    for op in range(2):
        x_wait(last, op)
        outputs(last, op)
    weight_grad(0, 1 - c)
    weight_grad(1, c)
    weight_grad(1, 1 - c)

    def add_up(w, carry):
        mine_at = pl.multiple_of(w * ROWS, ROWS)
        at = pl.ds(pl.multiple_of(w * PART, PART), PART)
        for op, out in ((0, lo), (1, gt)):
            total = ob[op, pl.ds(mine_at, PART), :].astype(F32)
            for n in range(1, 16):
                total = total + outr[op, n, at, :].astype(F32)
            out[at, :] = total.astype(BF)
        return carry

    for w in range(last):
        for op in range(2):
            wait_bytes(o_rows(w, op), o_rs.at[w, op])
    lax.fori_loop(0, last, add_up, 0)
    for op in range(2):
        wait_bytes(o_rows(last, op), o_rs.at[last, op])
    lax.fori_loop(last, WAVES, add_up, 0)

    for w in range(WAVES):
        messages = pl.ds(7 * w * CH, 7 * CH)
        for op in range(2):
            wait_bytes(cross_rows(w, op), a_ss.at[op, w])
            wait_bytes(relay_rows(w, op), r_ss.at[op, w])
            if w >= WAVES - 2:
                wait_bytes(px_ref(w, op), px_ss.at[w, op])
            wait_bytes(sb.at[op, messages], rs_ss.at[w, op])
            wait_bytes(sb.at[op, messages], ag_ss.at[w, op])
            wait_bytes(half_ref(w, op, c), x_ss.at[w, op])
            wait_bytes(o_rows(w, op), o_ss.at[w, op])


OUT_SHAPES = ((64, HALF), (64, HALF), (HALF, 2 * HALF), (2 * HALF, HALF))


def write_out(*refs):
    sems = refs[8]
    copies = []
    for i, rows in ((2, 96), (3, 192), (0, 64), (1, 64)):
        for at in range(0, OUT_SHAPES[i][0], rows):
            part = pl.ds(at, rows)
            copies.append(pltpu.make_async_copy(refs[i].at[part], refs[4 + i].at[part], sems.at[len(copies)]))
    for copy in copies:
        copy.start()
    for copy in copies:
        copy.wait()


def body(tokens, w_in, w_out, grad_out):
    dma = pltpu.SemaphoreType.DMA
    any_spec = pl.BlockSpec(memory_space=pl.ANY)
    results = pl.pallas_call(
        kernel,
        name="ffn",
        out_shape=tuple(pltpu.VMEM(shape, BF) for shape in OUT_SHAPES),
        in_specs=[any_spec] * 4,
        out_specs=[pl.BlockSpec(memory_space=pltpu.VMEM)] * 4,
        scratch_shapes=[
            pltpu.VMEM((2, 64, HALF), BF),
            pltpu.VMEM((2, 1024, HALF), BF),
            pltpu.VMEM((HALF, 2 * HALF), BF),
            pltpu.VMEM((2 * HALF, HALF), BF),
            pltpu.VMEM((2, 1024, HALF), F32),
            pltpu.VMEM((2, 2, 256, HALF), F32),
            pltpu.VMEM((2, 1024, HALF), F32),
            pltpu.VMEM((2, 7 * 128, HALF), BF),
            pltpu.VMEM((2, 7 * 128, HALF), BF),
            pltpu.VMEM((2, 2, 1024, HALF), BF),
            pltpu.VMEM((2, 1024, HALF), BF),
            pltpu.VMEM((2, 16, 64, HALF), BF),
            dma((4,)),
            dma((2, WAVES)), dma((2, WAVES)),
            dma((2, WAVES)), dma((2, WAVES)),
            dma((WAVES, 2)), dma((WAVES, 2)),
            dma((WAVES, 2)), dma((WAVES, 2, 7)),
            dma((WAVES, 2)), dma((WAVES, 2, 7)),
            dma((WAVES, 2)), dma((WAVES, 2)),
            dma((WAVES, 2)), dma((WAVES, 2)),
        ],
        compiler_params=pltpu.CompilerParams(
            collective_id=0, has_side_effects=True, vmem_limit_bytes=50 << 20
        ),
        cost_estimate=pl.CostEstimate(flops=14500000000, bytes_accessed=10000000, transcendentals=2000000),
    )(tokens, w_in, w_out, grad_out)
    return pl.pallas_call(
        write_out,
        name="write_out",
        out_shape=tuple(jax.ShapeDtypeStruct(shape, BF) for shape in OUT_SHAPES),
        in_specs=[any_spec] * 4,
        out_specs=[any_spec] * 4,
        compiler_params=pltpu.CompilerParams(vmem_limit_bytes=1 << 20),
        scratch_shapes=[dma((18,))],
        cost_estimate=pl.CostEstimate(flops=0, bytes_accessed=10000000, transcendentals=0),
    )(*[pltpu.with_memory_space_constraint(r, pltpu.VMEM) for r in results])


def solution(mesh):
    placed = (P("col", "row"), P("row", "col"), P("col", "row"), P("col", "row"))
    return jax.shard_map(
        body,
        mesh=mesh,
        in_specs=placed,
        out_specs=(P("col", "row"), P("col", "row"), P("row", "col"), P("col", "row")),
        check_vma=False,
    )
```

time: 509 us -> 118 us (0.23)
  waiting for transfers between devices: 445 us -> 0 us
  Pallas kernels: 0 us -> 117 us
  matrix products: 39.4 us -> 0 us
  between operations: 14.2 us -> 0.64 us
  other arithmetic: 5.28 us -> 0 us
    reduce_scatter x4 -> x0, waiting for transfers between devices: 267 us -> none  [the longest x1 82.2 us: body(): lax.psum_scatter(times_transposed(all_grad_hidden, w_in), 'col', scatter_...]
    all_gather x4 -> x0, waiting for transfers between devices: 176 us -> none  [the longest x1 53.3 us: body(): all_grads = lax.all_gather(grad_out, 'col', axis=0, tiled=True)]
    pallas_call x0 -> x2, Pallas kernels: none -> 117 us  [the longest x1 115 us: body(): pl.pallas_call(kernel, name='ffn', out_shape=tuple((pltpu.VMEM(shape, BF)...]
    dot_general x6 -> x0, matrix products: 39.4 us -> none  [the longest x2 13.5 us: times_plain(): return jnp.dot(left, right, preferred_element_type=jnp.float32)]
    convert_element_type x3 -> x0, other arithmetic: 5.28 us -> none  [the longest x1 2.12 us: body(): grad_hidden = (grad_act * gelu_slope(hidden)).astype(jnp.bfloat16)]
  transfers between devices with their start and end apart: 8 -> 0, of which waited for: 8 -> 0; matrix products, arithmetic and copies ran while one was open for 9% -> 0% of each run, Pallas kernels for 0% -> 0%
where the time goes in v2:
time: 118 us
  Pallas kernels  117 us (99%)
    pallas_call x1, Pallas kernels, body(): pl.pallas_call(kernel, name='ffn', out_shape=tuple((pltpu.VMEM(shape, BF)...  115 us
    pallas_call x1, Pallas kernels, body(): pl.pallas_call(write_out, name='write_out', out_shape=tuple((jax.ShapeDty...  2.38 us

profile of v2, /device:TPU:32, one launch (start us, length us, event | category | flops | bytes accessed | tf_op | source)
XLA Modules:
  0.0 117.5 jit_solution(17733468740097279772)
XLA Ops:
  0.6 114.5 %ffn.1 = (bf16[64,768]{1,0:T(8,128)(2,1)S(1)}, bf16[64,768]{1,0:T(8,128)(2,1)S(1)}, bf16[768,1536]{1,0:T(8,128)(2,1)S(1)}, bf16[1536,768]{1,0:T(8,128)(2,1)S(1)}) custom-call(bf16[64,768]{1,0:T(8,128)(2,1)} %tok_hbm.1, bf16[768,1536]{1,0:T(8,128)(2,1)} %win_hbm.1, bf16[1536,768]{1,0:T(8,128)(2,1)} %wout_hbm.1, bf16[64,768]{1,0:T(8,128)(2,1)} %gout_hbm.1), custom_call_target="tpu_custom_call" | custom-call | flops 14499999744 | bytes 10000000 | tf_op jit(solution)/shard_map/ffn/pallas_call | solution.py:394
  115.1 2.4 %write_out.1 = (bf16[64,768]{1,0:T(8,128)(2,1)}, bf16[64,768]{1,0:T(8,128)(2,1)}, bf16[768,1536]{1,0:T(8,128)(2,1)}, bf16[1536,768]{1,0:T(8,128)(2,1)}) custom-call(bf16[64,768]{1,0:T(8,128)(2,1)S(1)} %get-tuple-element.8.refs_0_, bf16[64,768]{1,0:T(8,128)(2,1)S(1)} %get-tuple-element.9.refs_1_, bf16[768,1536]{1,0:T(8,128)(2,1)S(1)} %get-tuple-element.10.refs_2_, ...), custom_call_target="tpu_custom_call" | custom-call | bytes 10000000 | tf_op jit(solution)/shard_map/write_out/pallas_call | solution.py:427

commit v3 on v2

--- a/solution.py
+++ b/solution.py
@@ -248,7 +248,31 @@
             return carry
 
         lax.fori_loop(0, HALF // TILE, tile, 0)
-        for n in (4, 1, 12, 3, 8, 2, 5, 15, 7, 13, 6, 9, 14, 11, 10):
+        push_outputs(w, op)
+
+    def outputs_half(op, half, finish):
+        w = WAVES - 1
+        tokens = ag.at[op, half, pl.ds(ROWS * w, ROWS)]
+        units = pl.ds(pl.multiple_of(half * HALF, HALF), HALF)
+
+        def tile(j, carry):
+            at = pl.ds(pl.multiple_of(j * TILE, TILE), TILE)
+            if op == 0:
+                total = dot_nn(tokens[...], w_out[units, at])
+            else:
+                total = dot_nt(tokens[...], w_in[at, units])
+            if finish:
+                ob[op, pl.ds(ROWS * w, ROWS), at] = (pown[op, pl.ds(0, ROWS), at] + total).astype(BF)
+            else:
+                pown[op, pl.ds(0, ROWS), at] = total
+            return carry
+
+        lax.fori_loop(0, HALF // TILE, tile, 0)
+        if finish:
+            push_outputs(w, op)
+
+    def push_outputs(w, op):
+        for n in (10, 6, 9, 14, 11, 5, 15, 7, 13, 8, 2, 4, 1, 12, 3):
             dy, dx = n // 4, n % 4
             remote(
                 ob.at[op, pl.ds(ROWS * w + part_of(dy, dx), PART)],
@@ -309,7 +333,7 @@
                 mine(w, 0)
                 mine(w, 1)
         for w in range(WAVES - 1):
-            if ages[w] == 9:
+            if ages[w] == 8:
                 for op in range(2):
                     x_wait(w, op)
                     outputs(w, op)
@@ -333,10 +357,12 @@
     for t in range(START[-1] + 9):
         tick(t)
     last = WAVES - 1
-    weight_grad(0, c)
+    for op in range(2):
+        outputs_half(op, c, False)
     for op in range(2):
         x_wait(last, op)
-        outputs(last, op)
+        outputs_half(op, 1 - c, True)
+    weight_grad(0, c)
     weight_grad(0, 1 - c)
     weight_grad(1, c)
     weight_grad(1, 1 - c)

time: 118 us -> 116 us (0.983); the launches traced: 118 us -> 114 us
  Pallas kernels: 117 us -> 113 us
    pallas_call x1, Pallas kernels: 115 us -> 111 us  [body(): pl.pallas_call(kernel, name='ffn', out_shape=tuple((pltpu.VMEM(shape, BF)...]
where the time goes in v3:
time: 116 us; the launch traced here: 114 us
  Pallas kernels  113 us (97%)
    pallas_call x1, Pallas kernels, body(): pl.pallas_call(kernel, name='ffn', out_shape=tuple((pltpu.VMEM(shape, BF)...  111 us
    pallas_call x1, Pallas kernels, body(): pl.pallas_call(write_out, name='write_out', out_shape=tuple((jax.ShapeDty...  2.38 us

profile of v3, /device:TPU:32, one launch (start us, length us, event | category | flops | bytes accessed | tf_op | source)
XLA Modules:
  0.0 113.7 jit_solution(2850671704213200368)
XLA Ops:
  0.6 110.7 %ffn.1 = (bf16[64,768]{1,0:T(8,128)(2,1)S(1)}, bf16[64,768]{1,0:T(8,128)(2,1)S(1)}, bf16[768,1536]{1,0:T(8,128)(2,1)S(1)}, bf16[1536,768]{1,0:T(8,128)(2,1)S(1)}) custom-call(bf16[64,768]{1,0:T(8,128)(2,1)} %tok_hbm.1, bf16[768,1536]{1,0:T(8,128)(2,1)} %win_hbm.1, bf16[1536,768]{1,0:T(8,128)(2,1)} %wout_hbm.1, bf16[64,768]{1,0:T(8,128)(2,1)} %gout_hbm.1), custom_call_target="tpu_custom_call" | custom-call | flops 14499999744 | bytes 10000000 | tf_op jit(solution)/shard_map/ffn/pallas_call | solution.py:420
  111.3 2.4 %write_out.1 = (bf16[64,768]{1,0:T(8,128)(2,1)}, bf16[64,768]{1,0:T(8,128)(2,1)}, bf16[768,1536]{1,0:T(8,128)(2,1)}, bf16[1536,768]{1,0:T(8,128)(2,1)}) custom-call(bf16[64,768]{1,0:T(8,128)(2,1)S(1)} %get-tuple-element.8.refs_0_, bf16[64,768]{1,0:T(8,128)(2,1)S(1)} %get-tuple-element.9.refs_1_, bf16[768,1536]{1,0:T(8,128)(2,1)S(1)} %get-tuple-element.10.refs_2_, ...), custom_call_target="tpu_custom_call" | custom-call | bytes 10000000 | tf_op jit(solution)/shard_map/write_out/pallas_call | solution.py:453

commit v4 on v3

--- a/solution.py
+++ b/solution.py
@@ -98,11 +98,11 @@
         pltpu.make_async_copy(ref, ref, sem).wait()
 
     def push_cross(w, arr):
-        for dy, dx in ((0, 1), (1, 0), (0, 3), (3, 0), (0, 2), (2, 0)):
+        for dy, dx in ((0, 2), (2, 0), (0, 1), (1, 0), (0, 3), (3, 0)):
             remote(
                 shard.at[arr, pl.ds(PART * w, PART)],
                 tg.at[arr, pl.ds(ROWS * w + part_of(dy, dx), PART)],
-                a_ss.at[arr, w],
+                a_ss.at[0],
                 a_rs.at[arr, w],
                 plane(-dy, -dx),
             ).start()
@@ -118,7 +118,7 @@
             remote(
                 tg.at[arr, pl.ds(ROWS * w + src, rows)],
                 tg.at[arr, pl.ds(ROWS * w + dst, rows)],
-                r_ss.at[arr, w],
+                r_ss.at[0],
                 r_rs.at[arr, w],
                 dev,
             ).start()
@@ -185,15 +185,16 @@
         return pl.ds((7 * w + n) * CH, CH)
 
     def rs_send(w, op, n):
-        k = z_chip(sign * (4 - n)) if n < 4 else z_chip(-sign * (7 - n))
+        way = sign if op == 0 else -sign
+        k = z_chip(way * (4 - n)) if n < 4 else z_chip(-way * (7 - n))
         term = own_term(w, op, k)
         if n not in (0, 4):
             wait_bytes(rb.at[op, slot(w, n - 1)], rs_rs.at[w, op, n - 1])
             term = term + rb[op, slot(w, n - 1), :].astype(F32)
         sb[op, slot(w, n), :] = term.astype(BF)
         remote(
-            sb.at[op, slot(w, n)], rb.at[op, slot(w, n)], rs_ss.at[w, op], rs_rs.at[w, op, n],
-            fwd if n < 4 else back,
+            sb.at[op, slot(w, n)], rb.at[op, slot(w, n)], rs_ss.at[0], rs_rs.at[w, op, n],
+            fwd if (n < 4) == (op == 0) else back,
         ).start()
 
     def rs_final(w, op):
@@ -216,11 +217,12 @@
         wait_bytes(sb.at[op, slot(w, n)], ag_rs.at[w, op, n])
 
     def ag_send(w, op, n):
-        k = z_chip(-sign * n) if n < 4 else z_chip(sign * (n - 4))
+        way = sign if op == 0 else -sign
+        k = z_chip(-way * n) if n < 4 else z_chip(way * (n - 4))
         if n not in (0, 4):
             ag_wait(w, op, n - 1)
         part = ag.at[op, c, chunk(w, k)]
-        remote(part, part, ag_ss.at[w, op], ag_rs.at[w, op, n], fwd if n < 4 else back).start()
+        remote(part, part, ag_ss.at[0], ag_rs.at[w, op, n], fwd if (n < 4) == (op == 0) else back).start()
 
     def half_ref(w, op, half):
         return ag.at[op, half, pl.ds(ROWS * w, ROWS)]
@@ -228,7 +230,7 @@
     def x_send(w, op):
         ag_wait(w, op, 6)
         ag_wait(w, op, 3)
-        remote(half_ref(w, op, c), half_ref(w, op, c), x_ss.at[w, op], x_rs.at[w, op], mate).start()
+        remote(half_ref(w, op, c), half_ref(w, op, c), x_ss.at[0], x_rs.at[w, op], mate).start()
 
     def x_wait(w, op):
         wait_bytes(half_ref(w, op, 1 - c), x_rs.at[w, op])
@@ -277,7 +279,7 @@
             remote(
                 ob.at[op, pl.ds(ROWS * w + part_of(dy, dx), PART)],
                 outr.at[op, n, pl.ds(PART * w, PART)],
-                o_ss.at[w, op],
+                o_ss.at[0],
                 o_rs.at[w, op],
                 plane(dy, dx),
             ).start()
@@ -385,17 +387,15 @@
         wait_bytes(o_rows(last, op), o_rs.at[last, op])
     lax.fori_loop(last, WAVES, add_up, 0)
 
-    for w in range(WAVES):
-        messages = pl.ds(7 * w * CH, 7 * CH)
+    wait_bytes(tg.at[0, pl.ds(0, 8 * 6 * PART)], a_ss.at[0])
+    wait_bytes(tg.at[:, pl.ds(0, 4 * 9 * PART)], r_ss.at[0])
+    wait_bytes(sb, rs_ss.at[0])
+    wait_bytes(sb, ag_ss.at[0])
+    wait_bytes(tg, x_ss.at[0])
+    wait_bytes(ob.at[:, pl.ds(0, 4 * 15 * PART)], o_ss.at[0])
+    for w in (WAVES - 2, WAVES - 1):
         for op in range(2):
-            wait_bytes(cross_rows(w, op), a_ss.at[op, w])
-            wait_bytes(relay_rows(w, op), r_ss.at[op, w])
-            if w >= WAVES - 2:
-                wait_bytes(px_ref(w, op), px_ss.at[w, op])
-            wait_bytes(sb.at[op, messages], rs_ss.at[w, op])
-            wait_bytes(sb.at[op, messages], ag_ss.at[w, op])
-            wait_bytes(half_ref(w, op, c), x_ss.at[w, op])
-            wait_bytes(o_rows(w, op), o_ss.at[w, op])
+            wait_bytes(px_ref(w, op), px_ss.at[w, op])
 
 
 OUT_SHAPES = ((64, HALF), (64, HALF), (HALF, 2 * HALF), (2 * HALF, HALF))
@@ -407,11 +407,11 @@
     for i, rows in ((2, 96), (3, 192), (0, 64), (1, 64)):
         for at in range(0, OUT_SHAPES[i][0], rows):
             part = pl.ds(at, rows)
-            copies.append(pltpu.make_async_copy(refs[i].at[part], refs[4 + i].at[part], sems.at[len(copies)]))
+            copies.append(pltpu.make_async_copy(refs[i].at[part], refs[4 + i].at[part], sems.at[i]))
     for copy in copies:
         copy.start()
-    for copy in copies:
-        copy.wait()
+    for i in range(4):
+        pltpu.make_async_copy(refs[i], refs[4 + i], sems.at[i]).wait()
 
 
 def body(tokens, w_in, w_out, grad_out):
@@ -437,13 +437,13 @@
             pltpu.VMEM((2, 1024, HALF), BF),
             pltpu.VMEM((2, 16, 64, HALF), BF),
             dma((4,)),
-            dma((2, WAVES)), dma((2, WAVES)),
-            dma((2, WAVES)), dma((2, WAVES)),
+            dma((1,)), dma((2, WAVES)),
+            dma((1,)), dma((2, WAVES)),
             dma((WAVES, 2)), dma((WAVES, 2)),
-            dma((WAVES, 2)), dma((WAVES, 2, 7)),
-            dma((WAVES, 2)), dma((WAVES, 2, 7)),
-            dma((WAVES, 2)), dma((WAVES, 2)),
-            dma((WAVES, 2)), dma((WAVES, 2)),
+            dma((1,)), dma((WAVES, 2, 7)),
+            dma((1,)), dma((WAVES, 2, 7)),
+            dma((1,)), dma((WAVES, 2)),
+            dma((1,)), dma((WAVES, 2)),
         ],
         compiler_params=pltpu.CompilerParams(
             collective_id=0, has_side_effects=True, vmem_limit_bytes=50 << 20
@@ -457,7 +457,7 @@
         in_specs=[any_spec] * 4,
         out_specs=[any_spec] * 4,
         compiler_params=pltpu.CompilerParams(vmem_limit_bytes=1 << 20),
-        scratch_shapes=[dma((18,))],
+        scratch_shapes=[dma((4,))],
         cost_estimate=pl.CostEstimate(flops=0, bytes_accessed=10000000, transcendentals=0),
     )(*[pltpu.with_memory_space_constraint(r, pltpu.VMEM) for r in results])
 

time: 116 us -> 114 us (0.983); the launches traced: 114 us -> 113 us
  no operation moved by 1% of the time
where the time goes in v4:
time: 114 us; the launch traced here: 113 us
  Pallas kernels  112 us (98%)
    pallas_call x1, Pallas kernels, body(): pl.pallas_call(kernel, name='ffn', out_shape=tuple((pltpu.VMEM(shape, BF)...  110 us

profile of v4, /device:TPU:32, one launch (start us, length us, event | category | flops | bytes accessed | tf_op | source)
XLA Modules:
  0.0 113.0 jit_solution(11461427827751461441)
XLA Ops:
  0.6 110.1 %ffn.1 = (bf16[64,768]{1,0:T(8,128)(2,1)S(1)}, bf16[64,768]{1,0:T(8,128)(2,1)S(1)}, bf16[768,1536]{1,0:T(8,128)(2,1)S(1)}, bf16[1536,768]{1,0:T(8,128)(2,1)S(1)}) custom-call(bf16[64,768]{1,0:T(8,128)(2,1)} %tok_hbm.1, bf16[768,1536]{1,0:T(8,128)(2,1)} %win_hbm.1, bf16[1536,768]{1,0:T(8,128)(2,1)} %wout_hbm.1, bf16[64,768]{1,0:T(8,128)(2,1)} %gout_hbm.1), custom_call_target="tpu_custom_call" | custom-call | flops 14499999744 | bytes 10000000 | tf_op jit(solution)/shard_map/ffn/pallas_call | solution.py:420
  110.8 2.3 %write_out.1 = (bf16[64,768]{1,0:T(8,128)(2,1)}, bf16[64,768]{1,0:T(8,128)(2,1)}, bf16[768,1536]{1,0:T(8,128)(2,1)}, bf16[1536,768]{1,0:T(8,128)(2,1)}) custom-call(bf16[64,768]{1,0:T(8,128)(2,1)S(1)} %get-tuple-element.8.refs_0_, bf16[64,768]{1,0:T(8,128)(2,1)S(1)} %get-tuple-element.9.refs_1_, bf16[768,1536]{1,0:T(8,128)(2,1)S(1)} %get-tuple-element.10.refs_2_, ...), custom_call_target="tpu_custom_call" | custom-call | bytes 10000000 | tf_op jit(solution)/shard_map/write_out/pallas_call | solution.py:453
